TPU v7x, 32 devices: a whole 2x2x4 slice. The times are simulated.
32 devices in a mesh: seq: 16 (over z, y, x), hid: 2 (over core).
Axes of the slice: x: 2, y: 2, z: 4, core: 2. Of those that a mesh axis runs over, the one named last changes fastest.
Arguments:
- tokens: bfloat16 [256, 6144], P('seq'), may hold values from -6 to 6
- out_grad: bfloat16 [256, 6144], P('seq'), may hold values from -6 to 6
- expert_ids: int32 [256, 2], P('seq'), may hold values from 0 to 7, all different within a row; in each aligned block of 16 rows (0 to 15, 16 to 31, ...) at most 5 rows name the same one
- route_probs: bfloat16 [256, 2], P('seq'), may hold values from 0.099609375 to 1
- w_gate: bfloat16 [6144, 32768], P(None, ('seq', 'hid')), may hold values from -0.078125 to 0.078125
- w_up: bfloat16 [6144, 32768], P(None, ('seq', 'hid')), may hold values from -0.078125 to 0.078125
- w_down: bfloat16 [32768, 6144], P(('seq', 'hid')), may hold values from -0.046875 to 0.046875
Outputs:
- grad_tokens: bfloat16 [256, 6144], P('seq', 'hid')
- grad_gate: bfloat16 [6144, 32768], P(None, ('seq', 'hid'))
- grad_up: bfloat16 [6144, 32768], P(None, ('seq', 'hid'))
- grad_down: bfloat16 [32768, 6144], P(('seq', 'hid'))
Inputs may be any that keep to these rules, and one draw needn't show every extreme that they name: `expert_ids`: within the rows of one index of seq, no expert is chosen by more than 5 rows, and some expert is chosen by exactly 5 of them in some such block.
All inputs are finite; a program needn't handle non-finite values.
Results may differ from a plain program's by a relative error of at most 0.005.
Values may be sent and summed in bfloat16 or wider, within the bound.
A program may use at most 128 MiB of HBM per device.

v0:
```python
import jax
import jax.numpy as jnp
from jax import lax
from jax.sharding import PartitionSpec as P

FF = 16384
TOPK = 2
EXP_WIN = 2


def silu_slope(gate_pre):
    sig_gate = jax.nn.sigmoid(gate_pre)
    return sig_gate * (1.0 + gate_pre * (1.0 - sig_gate))


def expert_block(tok_rows, grad_rows, row_weight, w_gate, w_up, w_down):
    gate_pre = jnp.dot(tok_rows, w_gate, preferred_element_type=jnp.float32)
    up_pre = jnp.dot(tok_rows, w_up, preferred_element_type=jnp.float32)
    act_val = jax.nn.silu(gate_pre)
    scaled = (row_weight * act_val * up_pre).astype(jnp.bfloat16)
    back_grad = lax.dot_general(
        grad_rows, w_down, (((1,), (1,)), ((), ())), preferred_element_type=jnp.float32
    )
    hidden_grad = row_weight * back_grad
    d_gate = (hidden_grad * up_pre * silu_slope(gate_pre)).astype(jnp.bfloat16)
    d_up = (hidden_grad * act_val).astype(jnp.bfloat16)
    return (d_gate, d_up, scaled)


def row_contract(left, right):
    return lax.dot_general(
        left, right, (((0,), (0,)), ((), ())), preferred_element_type=jnp.float32
    )


def col_contract(left, right):
    return lax.dot_general(
        left, right, (((1,), (1,)), ((), ())), preferred_element_type=jnp.float32
    )


def reduce_rows(term_fn, per_owner):
    row_sums = lax.psum_scatter(
        term_fn(jnp.int32(0), lax.axis_size("seq") * per_owner),
        "seq",
        scatter_dimension=0,
        tiled=True,
    )
    return lax.psum_scatter(row_sums, "hid", scatter_dimension=1, tiled=True)


def shards(tokens, out_grad, expert_ids, route_probs, w_gate, w_up, w_down):
    col_count = w_gate.shape[1]
    seq_count = lax.axis_size("seq")
    dev_block = lax.axis_index("seq") * lax.axis_size("hid") + lax.axis_index("hid")
    expert = dev_block * col_count // FF
    window = jnp.arange(EXP_WIN, dtype=jnp.int32)[None, :]
    combine = jnp.zeros((tokens.shape[0], EXP_WIN), jnp.float32)
    for pick_num in range(TOPK):
        combine = combine + jnp.where(
            expert_ids[:, pick_num : pick_num + 1] == window,
            route_probs[:, pick_num : pick_num + 1].astype(jnp.float32),
            0.0,
        )
    comb_own = combine.astype(jnp.bfloat16)
    tok_all, grad_all, comb_all = (
        lax.all_gather(tokens, "seq", axis=0, tiled=True),
        lax.all_gather(out_grad, "seq", axis=0, tiled=True),
        lax.all_gather(comb_own, "seq", axis=0, tiled=True),
    )
    row_weight = lax.dynamic_slice_in_dim(comb_all, expert, 1, 1).astype(jnp.float32)
    total_rows = tok_all.shape[0]
    own_rows = total_rows // seq_count
    d_gate, d_up, scaled = expert_block(tok_all, grad_all, row_weight, w_gate, w_up, w_down)
    grad_gate = row_contract(tok_all, d_gate)
    grad_up = row_contract(tok_all, d_up)
    grad_down = row_contract(scaled, grad_all)

    def row_term(row_start, row_count):
        return col_contract(d_gate, w_gate) + col_contract(d_up, w_up)

    grad_tokens = reduce_rows(row_term, own_rows)
    return (
        grad_tokens.astype(jnp.bfloat16),
        grad_gate.astype(jnp.bfloat16),
        grad_up.astype(jnp.bfloat16),
        grad_down.astype(jnp.bfloat16),
    )


def solution(mesh):
    return jax.shard_map(
        shards,
        mesh=mesh,
        in_specs=(
            P("seq", None),
            P("seq", None),
            P("seq", None),
            P("seq", None),
            P(None, ("seq", "hid")),
            P(None, ("seq", "hid")),
            P(("seq", "hid"), None),
        ),
        out_specs=(
            P("seq", "hid"),
            P(None, ("seq", "hid")),
            P(None, ("seq", "hid")),
            P(("seq", "hid"), None),
        ),
        check_vma=False,
    )
```

profile of v0, /device:TPU:0, one launch (start us, length us, event | category | flops | bytes accessed | tf_op | source)
XLA Modules:
  0.0 353.1 jit_solution(3236851439699150108)
XLA Ops:
  7.2 0.0 all-gather.6.cloned.1.call-start
  7.2 0.7 all-gather.6.cloned.1.call-update
  7.9 0.0 all-gather.4.cloned.1.call-start
  7.9 0.7 all-gather.4.cloned.1.call-update
  8.7 0.0 reduce-scatter.3.cloned.1.call-start
  8.7 0.7 bitcast_convert_fusion.1
  9.5 0.8 slice_bitcast_fusion.1
  10.2 42.2 %all-gather = bf16[16,16,2]{1,2,0:T(2,128)(2,1)S(1)} all-gather(bf16[1,16,2]{1,2,0:T(2,128)(2,1)S(1)} %fusion.5), channel_id=1, replica_groups=mesh['seq'=16,'hid'=2] {'seq'}, dimensions={0}, use_global_device_ids=true | all-gather | bytes 1088 | tf_op jit(solution)/shard_map/all_gather | solution.py:69
  52.5 0.1 reshape.12
  52.6 29.1 %all-gather.6.cloned.1.call-done = bf16[256,6144]{1,0:T(8,128)(2,1)} async-done(((bf16[16,6144]{1,0:T(8,128)(2,1)}), bf16[256,6144]{1,0:T(8,128)(2,1)}) %all-gather.6.cloned.1.call-update) | async-done | bytes 3145744 | tf_op jit(solution)/shard_map/all_gather | solution.py:67
  81.7 10.0 %fusion.8 = f32[256,1024]{1,0:T(8,128)} fusion(bf16[256,6144]{1,0:T(8,128)(2,1)} %all-gather.6.cloned.1.call-done, bf16[6144,1024]{1,0:T(8,128)(2,1)} %param.11), kind=kOutput, calls=%fused_computation.23 | convolution fusion | flops 3221225472 | bytes 16777216 | tf_op jit(solution)/shard_map/dot_general | solution.py:17
  91.7 0.0 copy-done
  91.7 7.4 %fusion.7 = f32[256,1024]{1,0:T(8,128)} fusion(bf16[256,6144]{1,0:T(8,128)(2,1)S(1)} %copy-done, bf16[6144,1024]{1,0:T(8,128)(2,1)} %param.12), kind=kOutput, calls=%fused_computation.22 | convolution fusion | flops 3221225472 | bytes 16777216 | tf_op jit(solution)/shard_map/dot_general | solution.py:18
  99.2 52.0 %all-gather.4.cloned.1.call-done = bf16[256,6144]{1,0:T(8,128)(2,1)} async-done(((bf16[16,6144]{1,0:T(8,128)(2,1)}), bf16[256,6144]{1,0:T(8,128)(2,1)}) %all-gather.4.cloned.1.call-update) | async-done | bytes 3145744 | tf_op jit(solution)/shard_map/all_gather | solution.py:68
  151.1 9.7 %multiply_convert_fusion.1 = (bf16[256,1024]{1,0:T(8,128)(2,1)S(1)}, bf16[256,1024]{1,0:T(8,128)(2,1)S(1)}) fusion(f32[256,1024]{1,0:T(8,128)} %fusion.8, f32[256,1024]{1,0:T(8,128)} %fusion.7, bf16[256,6144]{1,0:T(8,128)(2,1)} %all-gather.4.cloned.1.call-done, bf16[1024,6144]{1,0:T(8,128)(2,1)} %param.13, f32[256]{0:T(256)S(1)} %bitcast.34), kind=kOutput, calls=%fused_computation.6 | convolution fusion | flops 3224895488 | bytes 18875392 | tf_op jit(solution)/shard_map/dot_general | solution.py:21
  160.9 0.0 copy-start.3
  160.9 0.0 copy-start.2
  160.9 15.1 %fusion.9 = f32[256,6144]{1,0:T(8,128)} fusion(bf16[256,1024]{1,0:T(8,128)(2,1)S(1)} %get-tuple-element.17, bf16[6144,1024]{1,0:T(8,128)(2,1)} %param.11), kind=kOutput, calls=%fused_computation.24 | convolution fusion | flops 3221225472 | bytes 19398656 | tf_op jit(solution)/shard_map/dot_general | solution.py:37
  176.0 0.0 copy-done.3
  176.0 0.0 copy-done.2
  176.0 15.8 %convolution_add_fusion = f32[256,6144]{1,0:T(8,128)} fusion(f32[256,6144]{1,0:T(8,128)} %fusion.9, bf16[256,1024]{1,0:T(8,128)(2,1)S(1)} %get-tuple-element.16, bf16[6144,1024]{1,0:T(8,128)(2,1)} %param.12), kind=kOutput, calls=%fused_computation.3 | convolution fusion | flops 3222798336 | bytes 25690112 | tf_op jit(solution)/shard_map/dot_general | solution.py:37
  191.7 0.0 reduce-scatter.3.cloned.1.call-update
  191.8 0.0 reduce-scatter.5.cloned.1.call-start
  191.8 7.9 %convert_bitcast_fusion.1 = bf16[6144,1024]{0,1:T(8,128)(2,1)} fusion(bf16[256,1024]{1,0:T(8,128)(2,1)} %copy-done.3, bf16[256,6144]{1,0:T(8,128)(2,1)S(1)} %copy-done), kind=kOutput, calls=%fused_computation.1 | convolution fusion | flops 3227516928 | bytes 16252928 | tf_op jit(solution)/shard_map/dot_general | solution.py:31
  199.7 16.6 %copy.17 = bf16[6144,1024]{1,0:T(8,128)(2,1)} copy(bf16[6144,1024]{0,1:T(8,128)(2,1)} %convert_bitcast_fusion.1) | data formatting | bytes 25165824
  216.4 7.7 %convert_bitcast_fusion = bf16[6144,1024]{0,1:T(8,128)(2,1)} fusion(bf16[256,1024]{1,0:T(8,128)(2,1)} %copy-done.2, bf16[256,6144]{1,0:T(8,128)(2,1)S(1)} %copy-done), kind=kOutput, calls=%fused_computation | convolution fusion | flops 3227516928 | bytes 16252928 | tf_op jit(solution)/shard_map/dot_general | solution.py:31
  224.0 16.8 %copy.18 = bf16[6144,1024]{1,0:T(8,128)(2,1)} copy(bf16[6144,1024]{0,1:T(8,128)(2,1)} %convert_bitcast_fusion) | data formatting | bytes 25165824
  240.8 95.1 %reduce-scatter.3.cloned.1.call-done = f32[16,6144]{1,0:T(8,128)} async-done(((f32[256,6144]{1,0:T(8,128)}), f32[16,6144]{1,0:T(8,128)}) %reduce-scatter.3.cloned.1.call-update) | async-done | bytes 393232 | tf_op jit(solution)/shard_map/reduce_scatter | solution.py:43
  336.0 0.0 reduce-scatter.5.cloned.1.call-update
  336.0 8.3 %convolution_convert_fusion = bf16[1024,6144]{1,0:T(8,128)(2,1)} fusion(bf16[256,6144]{1,0:T(8,128)(2,1)S(1)} %copy-done.1, f32[256,1024]{1,0:T(8,128)} %fusion.7, f32[256]{0:T(256)S(1)} %bitcast.35, f32[256,1024]{1,0:T(8,128)} %fusion.8), kind=kOutput, calls=%fused_computation.2 | convolution fusion | flops 3229351936 | bytes 17826816 | tf_op jit(solution)/shard_map/dot_general | solution.py:31
  344.3 0.7 reduce-scatter.5.cloned.1.call-done
  345.0 1.6 convert_element_type.36
  (6 shorter events, 0.0 us)
Async XLA Ops:
  7.2 74.5 %all-gather.6.cloned.1.call-start = ((), (), s32[]{:S(2)}) async-start(), calls=%async_computation.3 | async-start | bytes 3342336 | tf_op jit(solution)/shard_map/all_gather | solution.py:67
  7.9 143.2 %all-gather.4.cloned.1.call-start = ((), (), s32[]{:S(2)}) async-start(), calls=%async_computation.2 | async-start | bytes 3342336 | tf_op jit(solution)/shard_map/all_gather | solution.py:68
  8.7 327.3 %reduce-scatter.3.cloned.1.call-start = ((), (), s32[]{:S(2)}) async-start(), calls=%async_computation.4 | async-start | bytes 6684672 | tf_op jit(solution)/shard_map/reduce_scatter | solution.py:43
  81.7 10.0 %copy-start = (bf16[256,6144]{1,0:T(8,128)(2,1)S(1)}, bf16[256,6144]{1,0:T(8,128)(2,1)}, u32[]{:S(2)}) copy-start(bf16[256,6144]{1,0:T(8,128)(2,1)} %all-gather.6.cloned.1.call-done) | copy-start | bytes 9437188
  160.9 15.1 %copy-start.3 = (bf16[256,1024]{1,0:T(8,128)(2,1)}, bf16[256,1024]{1,0:T(8,128)(2,1)S(1)}, u32[]{:S(2)}) copy-start(bf16[256,1024]{1,0:T(8,128)(2,1)S(1)} %get-tuple-element.17) | copy-start | bytes 1572868
  160.9 15.1 %copy-start.2 = (bf16[256,1024]{1,0:T(8,128)(2,1)}, bf16[256,1024]{1,0:T(8,128)(2,1)S(1)}, u32[]{:S(2)}) copy-start(bf16[256,1024]{1,0:T(8,128)(2,1)S(1)} %get-tuple-element.16) | copy-start | bytes 1572868
  191.8 153.2 %reduce-scatter.5.cloned.1.call-start = ((), (), s32[]{:S(2)}) async-start(), calls=%async_computation.5 | async-start | bytes 589824 | tf_op jit(solution)/shard_map/reduce_scatter | solution.py:49
  224.0 112.0 %copy-start.1 = (bf16[256,6144]{1,0:T(8,128)(2,1)S(1)}, bf16[256,6144]{1,0:T(8,128)(2,1)}, u32[]{:S(2)}) copy-start(bf16[256,6144]{1,0:T(8,128)(2,1)} %all-gather.4.cloned.1.call-done) | copy-start | bytes 9437188
Sparse Core Ops, SparseCore 0:
  10.8 70.8 all-gather.5
  84.5 66.6 all-gather.3
  191.9 144.0 reduce-scatter.2
  338.1 6.8 reduce-scatter.4
where the time goes:
time: 354 us; the launch traced here: 353 us
  waiting for transfers between devices  178 us (50%)
  matrix products  81.9 us (23%)
  blocking collectives  42.2 us (12%)
  local copies, waits for them, and re-layouts  34.3 us (10%)
  between operations  13.8 us (4%)
    reduce_scatter x1, waiting for transfers between devices, reduce_rows(): lax.psum_scatter(term_fn(jnp.int32(0), lax.axis_size('seq') * per_owner),...  95.1 us
    all_gather x1, waiting for transfers between devices, shards(): lax.all_gather(out_grad, 'seq', axis=0, tiled=True)  52 us
    all_gather x1, blocking collectives, shards(): lax.all_gather(comb_own, 'seq', axis=0, tiled=True)  42.2 us
    unnamed x11, local copies, waits for them, and re-layouts  33.6 us
    dot_general x2, matrix products, col_contract(): lax.dot_general(left, right, (((1,), (1,)), ((), ())), preferred_element_...  30.8 us
    all_gather x1, waiting for transfers between devices, shards(): lax.all_gather(tokens, 'seq', axis=0, tiled=True)  29.1 us
    dot_general x3, matrix products, row_contract(): lax.dot_general(left, right, (((0,), (0,)), ((), ())), preferred_element_...  23.9 us
    dot_general x1, matrix products, expert_block(): gate_pre = jnp.dot(tok_rows, w_gate, preferred_element_type=jnp.float32)  10 us
  transfers between devices with their start and end apart: 4, of which 4 were waited for; matrix products, arithmetic and copies ran while one was open for 22% of the time, Pallas kernels for 0%

commit v1 on v0

v1 whole, which is shorter than its diff:
```python
import functools

import jax
import jax.numpy as jnp
from jax import lax
from jax.experimental import pallas as pl
from jax.experimental.pallas import tpu as pltpu
from jax.sharding import PartitionSpec as P

FF = 16384
TOPK = 2
EXP_WIN = 2
MOST = 5
LANES = 128
SLAB = 16
PIECES = 3
MESH = pl.DeviceIdType.MESH
F32 = jnp.float32
BF16 = jnp.bfloat16


def silu_slope(gate_pre):
    sig_gate = jax.nn.sigmoid(gate_pre)
    return sig_gate * (1.0 + gate_pre * (1.0 - sig_gate))


def row_contract(left, right):
    return lax.dot_general(
        left, right, (((0,), (0,)), ((), ())), preferred_element_type=F32
    )


def col_contract(left, right):
    return lax.dot_general(
        left, right, (((1,), (1,)), ((), ())), preferred_element_type=F32
    )


def dot(left, right):
    return jnp.dot(left, right, preferred_element_type=F32)


def iota(shape, axis):
    return lax.broadcasted_iota(jnp.int32, shape, axis)


def expert_block(tok_rows, grad_rows, row_weight, w_gate, w_up, w_down):
    gate_pre = dot(tok_rows, w_gate)
    up_pre = dot(tok_rows, w_up)
    act_val = jax.nn.silu(gate_pre)
    scaled = (row_weight * act_val * up_pre).astype(BF16)
    hidden_grad = row_weight * col_contract(grad_rows, w_down)
    d_gate = (hidden_grad * up_pre * silu_slope(gate_pre)).astype(BF16)
    d_up = (hidden_grad * act_val).astype(BF16)
    return (d_gate, d_up, scaled)


def plain_shards(tokens, out_grad, expert_ids, route_probs, w_gate, w_up, w_down):
    col_count = w_gate.shape[1]
    dev_block = lax.axis_index("seq") * lax.axis_size("hid") + lax.axis_index("hid")
    expert = dev_block * col_count // FF
    window = jnp.arange(EXP_WIN, dtype=jnp.int32)[None, :]
    combine = jnp.zeros((tokens.shape[0], EXP_WIN), F32)
    for pick_num in range(TOPK):
        combine = combine + jnp.where(
            expert_ids[:, pick_num : pick_num + 1] == window,
            route_probs[:, pick_num : pick_num + 1].astype(F32),
            0.0,
        )
    tok_all, grad_all, comb_all = (
        lax.all_gather(tokens, "seq", axis=0, tiled=True),
        lax.all_gather(out_grad, "seq", axis=0, tiled=True),
        lax.all_gather(combine.astype(BF16), "seq", axis=0, tiled=True),
    )
    row_weight = lax.dynamic_slice_in_dim(comb_all, expert, 1, 1).astype(F32)
    d_gate, d_up, scaled = expert_block(
        tok_all, grad_all, row_weight, w_gate, w_up, w_down
    )
    terms = col_contract(d_gate, w_gate) + col_contract(d_up, w_up)
    row_sums = lax.psum_scatter(terms, "seq", scatter_dimension=0, tiled=True)
    grad_tokens = lax.psum_scatter(row_sums, "hid", scatter_dimension=1, tiled=True)
    return (
        grad_tokens.astype(BF16),
        row_contract(tok_all, d_gate).astype(BF16),
        row_contract(tok_all, d_up).astype(BF16),
        row_contract(scaled, grad_all).astype(BF16),
    )


def unpack_rows(seq_count, piece):
    rows, packed = MOST * seq_count, SLAB * seq_count
    n, r = iota((rows, packed), 0), iota((rows, packed), 1)
    return (r == SLAB * (n % seq_count) + MOST * piece + n // seq_count).astype(BF16)


def pack_rows(seq_count, piece):
    rows, packed = MOST * seq_count, SLAB * seq_count
    r, n = iota((packed, rows), 0), iota((packed, rows), 1)
    return (r == SLAB * (n % seq_count) + MOST * piece + n // seq_count).astype(BF16)


def layer_kernel(
    group,
    tok_ref,
    grad_ref,
    ids_ref,
    probs_ref,
    wg_hbm,
    wu_hbm,
    wd_hbm,
    out_ref,
    dg_ref,
    du_ref,
    sc_ref,
    tokx_ref,
    gradx_ref,
    wg,
    wu,
    wd,
    slabs,
    mir,
    gate,
    up,
    back,
    sib_out,
    sib_in,
    packed,
    red_in,
    total,
    fin_out,
    fin_in,
    w_sem,
    mir_sem,
    gat_send,
    gat_recv,
    sib_sem,
    part_sem,
    red_send,
    red_recv,
    fin_sem,
):
    seq_count = EXP_WIN * group
    rows_own, width = tok_ref.shape
    half_width = width // 2
    piece_w = half_width // PIECES
    hidden = wg.shape[2]
    me, h = lax.axis_index("seq"), lax.axis_index("hid")
    mine, c = me // group, me % group
    other = 1 - mine
    mirror = (me + group) % seq_count
    sib = (me, 1 - h)

    def weight_copies(i):
        return (
            pltpu.make_async_copy(
                wg_hbm.at[pl.ds(i * piece_w, piece_w), :], wg.at[i], w_sem.at[0, i]
            ),
            pltpu.make_async_copy(
                wu_hbm.at[pl.ds(i * piece_w, piece_w), :], wu.at[i], w_sem.at[1, i]
            ),
            pltpu.make_async_copy(
                wd_hbm.at[:, pl.ds(pl.multiple_of(i * piece_w, LANES), piece_w)],
                wd.at[i],
                w_sem.at[2, i],
            ),
        )

    def order(t):
        return ((h + t // PIECES) % 2) * PIECES + t % PIECES

    def start_gate_up(t, _):
        copies = weight_copies(order(t))
        copies[0].start()
        copies[1].start()
        return 0

    def start_down(t, _):
        weight_copies(order(t))[2].start()
        return 0

    lax.fori_loop(0, 2 * PIECES, start_gate_up, 0)
    lax.fori_loop(0, 2 * PIECES, start_down, 0)

    barrier = pltpu.get_barrier_semaphore()

    def greet(d, _):
        pl.semaphore_signal(
            barrier,
            inc=1,
            device_id=(mine * group + (c + d) % group, h),
            device_id_type=MESH,
        )
        return 0

    lax.fori_loop(1, group, greet, 0)
    pl.semaphore_signal(barrier, inc=1, device_id=(mirror, h), device_id_type=MESH)
    pl.semaphore_signal(barrier, inc=1, device_id=sib, device_id_type=MESH)

    below = (iota((rows_own, rows_own), 1) < iota((rows_own, rows_own), 0)).astype(BF16)

    def chosen(expert):
        weight = jnp.zeros((rows_own, 1), F32)
        hit = jnp.zeros((rows_own, 1), F32)
        for pick in range(TOPK):
            same = ids_ref[:, pick : pick + 1] == expert
            hit = hit + jnp.where(same, 1.0, 0.0)
            weight = weight + jnp.where(
                same, probs_ref[:, pick : pick + 1].astype(F32), 0.0
            )
        spread = jnp.broadcast_to(hit, (rows_own, LANES)).astype(BF16)
        place = dot(below, spread)[:, 0:1]
        place = jnp.where(hit > 0.0, place, -1.0)
        return place, weight

    def picker(place, piece):
        r = iota((rows_own, SLAB), 1) - MOST * piece
        inside = (r >= 0) & (r < MOST)
        return jnp.where(inside & (r.astype(F32) == place), 1.0, 0.0).astype(BF16)

    def slab_of(x_ref, place):
        acc = jnp.zeros((SLAB, piece_w), F32)
        for piece in range(PIECES):
            start = pl.multiple_of(h * half_width + piece * piece_w, LANES)
            acc = acc + row_contract(picker(place, piece), x_ref[:, pl.ds(start, piece_w)])
        return acc

    def token_slab(place, weight):
        spot = (iota((rows_own, piece_w), 1) // LANES).astype(F32)
        line = jnp.sum(jnp.where(spot == place, weight, 0.0), axis=0, keepdims=True)
        return jnp.where(
            iota((SLAB, piece_w), 0) == SLAB - 1, line, slab_of(tok_ref, place)
        )

    place_mine, weight_mine = chosen(mine)
    place_other, weight_other = chosen(other)
    mir[0] = token_slab(place_other, weight_other).astype(BF16)
    mir[1] = slab_of(grad_ref, place_other).astype(BF16)
    own_rows = pl.ds(pl.multiple_of(2 * SLAB * c + SLAB * mine, SLAB), SLAB)
    mir_rows = pl.ds(pl.multiple_of(2 * SLAB * c + SLAB * other, SLAB), SLAB)
    slabs[0, h, own_rows, :] = token_slab(place_mine, weight_mine).astype(BF16)
    slabs[1, h, own_rows, :] = slab_of(grad_ref, place_mine).astype(BF16)

    pl.semaphore_wait(barrier, group + 1)

    def mirror_copy(a, rows):
        return pltpu.make_async_remote_copy(
            src_ref=mir.at[a],
            dst_ref=slabs.at[a, h, rows, :],
            send_sem=mir_sem.at[0, a],
            recv_sem=mir_sem.at[1, a],
            device_id=(mirror, h),
            device_id_type=MESH,
        )

    def gather_copy(a, part, d, source):
        row = 2 * SLAB * source + SLAB * (mine if part == 0 else other)
        rows = pl.ds(pl.multiple_of(row, SLAB), SLAB)
        return pltpu.make_async_remote_copy(
            src_ref=slabs.at[a, h, rows, :],
            dst_ref=slabs.at[a, h, rows, :],
            send_sem=gat_send.at[a, part, d],
            recv_sem=gat_recv.at[a, part, d],
            device_id=(mine * group + (c + d) % group, h),
            device_id_type=MESH,
        )

    def send_all(a, part):
        def step(d, _):
            gather_copy(a, part, d, c).start()
            return 0

        lax.fori_loop(1, group, step, 0)

    def receive_all(a):
        def step(d, _):
            source = (c + group - d) % group
            gather_copy(a, 0, d, source).wait_recv()
            gather_copy(a, 1, d, source).wait_recv()
            return 0

        lax.fori_loop(1, group, step, 0)

    def pair_copy(a, half):
        return pltpu.make_async_remote_copy(
            src_ref=slabs.at[a, half],
            dst_ref=slabs.at[a, half],
            send_sem=sib_sem.at[0, a],
            recv_sem=sib_sem.at[1, a],
            device_id=sib,
            device_id_type=MESH,
        )

    mirror_copy(0, own_rows).start()
    mirror_copy(1, own_rows).start()
    send_all(0, 0)
    mirror_copy(0, mir_rows).wait_recv()
    send_all(0, 1)
    send_all(1, 0)
    mirror_copy(1, mir_rows).wait_recv()
    send_all(1, 1)

    receive_all(0)
    pair_copy(0, h).start()

    rows_all = MOST * seq_count
    n, r = iota((rows_all, SLAB * seq_count), 0), iota((rows_all, SLAB * seq_count), 1)
    last = (r == SLAB * (n % seq_count) + SLAB - 1).astype(BF16)
    lines = dot(last, slabs[0, h])
    n, r = iota((rows_all, piece_w), 0), iota((rows_all, piece_w), 1)
    row_weight = jnp.sum(
        jnp.where(r == LANES * (n // seq_count), lines, 0.0), axis=1, keepdims=True
    )

    gate[...] = jnp.zeros_like(gate)
    up[...] = jnp.zeros_like(up)
    back[...] = jnp.zeros_like(back)

    def rows_of(a, i, x_ref):
        x = dot(unpack_rows(seq_count, i % PIECES), slabs[a, i // PIECES]).astype(BF16)
        x_ref[:, pl.ds(pl.multiple_of(i * piece_w, LANES), piece_w)] = x
        return x

    def forward_step(t, _):
        i = order(t)
        copies = weight_copies(i)
        x = rows_of(0, i, tokx_ref)
        copies[0].wait()
        gate[...] += dot(x, wg[i])
        copies[1].wait()
        up[...] += dot(x, wu[i])
        return 0

    def back_step(t, _):
        i = order(t)
        x = rows_of(1, i, gradx_ref)
        weight_copies(i)[2].wait()
        back[...] += col_contract(x, wd[i])
        return 0

    lax.fori_loop(0, PIECES, forward_step, 0)
    receive_all(1)
    pair_copy(1, h).start()
    pair_copy(0, 1 - h).wait_recv()
    lax.fori_loop(PIECES, 2 * PIECES, forward_step, 0)
    lax.fori_loop(0, PIECES, back_step, 0)
    pair_copy(1, 1 - h).wait_recv()
    lax.fori_loop(PIECES, 2 * PIECES, back_step, 0)

    gate_pre, up_pre = gate[...], up[...]
    sig = 1.0 / (1.0 + jnp.exp(-gate_pre))
    act = gate_pre * sig
    hidden_grad = row_weight * back[...]
    sc_ref[...] = (row_weight * act * up_pre).astype(BF16)
    dg_ref[...] = (
        hidden_grad * up_pre * (sig * (1.0 + gate_pre * (1.0 - sig)))
    ).astype(BF16)
    du_ref[...] = (hidden_grad * act).astype(BF16)

    cuts = packed.shape[0]
    cut = piece_w // cuts

    def terms(half, q, piece):
        i = half * PIECES + piece
        rows = pl.ds(pl.multiple_of(q * cut, SLAB), cut)
        return col_contract(dg_ref[...], wg[i, rows, :]) + col_contract(
            du_ref[...], wu[i, rows, :]
        )

    def part_copy(q):
        return pltpu.make_async_remote_copy(
            src_ref=sib_out.at[q],
            dst_ref=sib_in.at[q],
            send_sem=part_sem.at[0, q],
            recv_sem=part_sem.at[1, q],
            device_id=sib,
            device_id_type=MESH,
        )

    def reduce_copy(q, d):
        target = (c + d) % group
        return pltpu.make_async_remote_copy(
            src_ref=packed.at[
                q, pl.ds(pl.multiple_of(2 * SLAB * target, 2 * SLAB), 2 * SLAB), :
            ],
            dst_ref=red_in.at[q, d],
            send_sem=red_send.at[q, d],
            recv_sem=red_recv.at[q, d],
            device_id=(mine * group + target, h),
            device_id_type=MESH,
        )

    def far_step(q, _):
        for piece in range(PIECES):
            sib_out[q, piece] = terms(1 - h, q, piece).astype(BF16)
        part_copy(q).start()
        return 0

    def near_step(q, _):
        part_copy(q).wait_recv()
        acc = jnp.zeros((SLAB * seq_count, cut), F32)
        for piece in range(PIECES):
            both = terms(h, q, piece) + sib_in[q, piece].astype(F32)
            acc = acc + dot(pack_rows(seq_count, piece), both.astype(BF16))
        packed[q] = acc.astype(BF16)

        def send(d, _):
            reduce_copy(q, d).start()
            return 0

        lax.fori_loop(1, group, send, 0)
        return 0

    lax.fori_loop(0, cuts, far_step, 0)
    lax.fori_loop(0, cuts, near_step, 0)

    def final_copy(q):
        return pltpu.make_async_remote_copy(
            src_ref=fin_out.at[q],
            dst_ref=fin_in.at[q],
            send_sem=fin_sem.at[0, q],
            recv_sem=fin_sem.at[1, q],
            device_id=(mirror, h),
            device_id_type=MESH,
        )

    def sum_step(q, _):
        own = pl.ds(pl.multiple_of(2 * SLAB * c, 2 * SLAB), 2 * SLAB)
        total[q] = packed[q, own, :].astype(F32)

        def add(d, _):
            reduce_copy(q, d).wait_recv()
            total[q] += red_in[q, d].astype(F32)
            return 0

        lax.fori_loop(1, group, add, 0)
        away = pl.ds(pl.multiple_of(SLAB * other, SLAB), SLAB)
        fin_out[q] = total[q, away, :].astype(BF16)
        final_copy(q).start()
        return 0

    lax.fori_loop(0, cuts, sum_step, 0)

    stay = pl.ds(pl.multiple_of(SLAB * mine, SLAB), SLAB)
    for q in range(cuts):
        final_copy(q).wait_recv()
        near = total[q, stay, :].astype(BF16)
        far = fin_in[q]
        for piece in range(PIECES):
            value = dot(picker(place_mine, piece), near) + dot(
                picker(place_other, piece), far
            )
            out_ref[:, piece * piece_w + q * cut : piece * piece_w + (q + 1) * cut] = (
                value.astype(BF16)
            )

    for a in range(2):
        mirror_copy(a, own_rows).wait_send()
        pair_copy(a, h).wait_send()

    def sent(d, _):
        for a in range(2):
            for part in range(2):
                gather_copy(a, part, d, c).wait_send()
        for q in range(cuts):
            reduce_copy(q, d).wait_send()
        return 0

    lax.fori_loop(1, group, sent, 0)
    for q in range(cuts):
        part_copy(q).wait_send()
        final_copy(q).wait_send()


def weight_grads(tokx_ref, gradx_ref, dg_ref, du_ref, sc_ref, gg_ref, gu_ref, gd_ref):
    x = tokx_ref[...]
    gg_ref[...] = row_contract(x, dg_ref[...]).astype(BF16)
    gu_ref[...] = row_contract(x, du_ref[...]).astype(BF16)
    gd_ref[...] = row_contract(sc_ref[...], gradx_ref[...]).astype(BF16)


def paired_shards(group, tokens, out_grad, expert_ids, route_probs, w_gate, w_up, w_down):
    seq_count = EXP_WIN * group
    rows = MOST * seq_count
    width, hidden = w_gate.shape
    piece_w = width // (2 * PIECES)
    cuts = 2
    cut = piece_w // cuts
    dma = pltpu.SemaphoreType.DMA
    vmem = pl.BlockSpec(memory_space=pltpu.VMEM)
    hbm = pl.BlockSpec(memory_space=pl.ANY)
    small = jax.ShapeDtypeStruct((rows, hidden), BF16)
    wide = jax.ShapeDtypeStruct((rows, width), BF16)
    grad_tokens, d_gate, d_up, scaled, tok_x, grad_x = pl.pallas_call(
        functools.partial(layer_kernel, group),
        out_shape=(
            jax.ShapeDtypeStruct((tokens.shape[0], width // 2), BF16),
            small,
            small,
            small,
            wide,
            wide,
        ),
        in_specs=[vmem] * 4 + [hbm] * 3,
        out_specs=(vmem,) * 6,
        scratch_shapes=[
            pltpu.VMEM((2 * PIECES, piece_w, hidden), BF16),
            pltpu.VMEM((2 * PIECES, piece_w, hidden), BF16),
            pltpu.VMEM((2 * PIECES, hidden, piece_w), BF16),
            pltpu.VMEM((2, 2, SLAB * seq_count, piece_w), BF16),
            pltpu.VMEM((2, SLAB, piece_w), BF16),
            pltpu.VMEM((rows, hidden), F32),
            pltpu.VMEM((rows, hidden), F32),
            pltpu.VMEM((rows, hidden), F32),
            pltpu.VMEM((cuts, PIECES, rows, cut), BF16),
            pltpu.VMEM((cuts, PIECES, rows, cut), BF16),
            pltpu.VMEM((cuts, SLAB * seq_count, cut), BF16),
            pltpu.VMEM((cuts, group, 2 * SLAB, cut), BF16),
            pltpu.VMEM((cuts, 2 * SLAB, cut), F32),
            pltpu.VMEM((cuts, SLAB, cut), BF16),
            pltpu.VMEM((cuts, SLAB, cut), BF16),
            dma((3, 2 * PIECES)),
            dma((2, 2)),
            dma((2, 2, group)),
            dma((2, 2, group)),
            dma((2, 2)),
            dma((2, cuts)),
            dma((cuts, group)),
            dma((cuts, group)),
            dma((2, cuts)),
        ],
        compiler_params=pltpu.CompilerParams(
            collective_id=0, has_side_effects=True, vmem_limit_bytes=60 * 2**20
        ),
        cost_estimate=pl.CostEstimate(
            flops=10 * rows * width * hidden,
            bytes_accessed=6 * width * hidden,
            transcendentals=rows * hidden,
        ),
    )(tokens, out_grad, expert_ids, route_probs, w_gate, w_up, w_down)

    step = piece_w // 2
    whole = pl.BlockSpec((rows, hidden), lambda i: (0, 0))
    strip = pl.BlockSpec((rows, step), lambda i: (0, i))
    grad_gate, grad_up, grad_down = pl.pallas_call(
        weight_grads,
        grid=(width // step,),
        out_shape=(
            jax.ShapeDtypeStruct((width, hidden), BF16),
            jax.ShapeDtypeStruct((width, hidden), BF16),
            jax.ShapeDtypeStruct((hidden, width), BF16),
        ),
        in_specs=[strip, strip, whole, whole, whole],
        out_specs=(
            pl.BlockSpec((step, hidden), lambda i: (i, 0)),
            pl.BlockSpec((step, hidden), lambda i: (i, 0)),
            pl.BlockSpec((hidden, step), lambda i: (0, i)),
        ),
        compiler_params=pltpu.CompilerParams(vmem_limit_bytes=48 * 2**20),
        cost_estimate=pl.CostEstimate(
            flops=6 * rows * width * hidden,
            bytes_accessed=6 * width * hidden,
            transcendentals=0,
        ),
    )(tok_x, grad_x, d_gate, d_up, scaled)
    return grad_tokens, grad_gate, grad_up, grad_down


def solution(mesh):
    paired = mesh.shape["hid"] == 2 and mesh.shape["seq"] % EXP_WIN == 0
    if paired:
        body = functools.partial(paired_shards, mesh.shape["seq"] // EXP_WIN)
    else:
        body = plain_shards
    return jax.shard_map(
        body,
        mesh=mesh,
        in_specs=(
            P("seq", None),
            P("seq", None),
            P("seq", None),
            P("seq", None),
            P(None, ("seq", "hid")),
            P(None, ("seq", "hid")),
            P(("seq", "hid"), None),
        ),
        out_specs=(
            P("seq", "hid"),
            P(None, ("seq", "hid")),
            P(None, ("seq", "hid")),
            P(("seq", "hid"), None),
        ),
        check_vma=False,
    )
```

time: 354 us -> 76.4 us (0.22)
  waiting for transfers between devices: 178 us -> 0 us
  matrix products: 81.9 us -> 0 us
  Pallas kernels: 0 us -> 66.1 us
  blocking collectives: 42.2 us -> 0 us
  local copies, waits for them, and re-layouts: 34.3 us -> 9.36 us
  between operations: 13.8 us -> 0.65 us
    reduce_scatter x2 -> x0, waiting for transfers between devices: 95.8 us -> none  [the longest x1 95.1 us: reduce_rows(): lax.psum_scatter(term_fn(jnp.int32(0), lax.axis_size('seq') * per_owner),...]
    dot_general x8 -> x0, matrix products: 81.9 us -> none  [the longest x2 30.8 us: col_contract(): lax.dot_general(left, right, (((1,), (1,)), ((), ())), preferred_element_...]
    all_gather x2 -> x0, waiting for transfers between devices: 81.1 us -> none  [the longest x1 52 us: shards(): lax.all_gather(out_grad, 'seq', axis=0, tiled=True)]
    pallas_call x0 -> x2, Pallas kernels: none -> 66.1 us  [the longest x1 50.9 us: paired_shards(): pl.pallas_call(functools.partial(layer_kernel, group), out_shape=(jax.Sha...]
    all_gather x1 -> x0, blocking collectives: 42.2 us -> none  [shards(): lax.all_gather(comb_own, 'seq', axis=0, tiled=True)]
    unnamed x11 -> x13, local copies, waits for them, and re-layouts: 33.6 us -> 9.36 us
  transfers between devices with their start and end apart: 4 -> 0, of which waited for: 4 -> 0; matrix products, arithmetic and copies ran while one was open for 22% -> 0% of each run, Pallas kernels for 0% -> 0%
where the time goes in v1:
time: 76.4 us; the launch traced here: 76.1 us
  Pallas kernels  66.1 us (87%)
  local copies, waits for them, and re-layouts  9.36 us (12%)
    pallas_call x1, Pallas kernels, paired_shards(): pl.pallas_call(functools.partial(layer_kernel, group), out_shape=(jax.Sha...  50.9 us
    pallas_call x1, Pallas kernels, paired_shards(): pl.pallas_call(weight_grads, grid=(width // step,), out_shape=(jax.ShapeD...  15.2 us
    unnamed x13, local copies, waits for them, and re-layouts  9.36 us

profile of v1, /device:TPU:0, one launch (start us, length us, event | category | flops | bytes accessed | tf_op | source)
XLA Modules:
  0.0 76.1 jit_solution(14816455620797630270)
XLA Ops:
  0.6 1.3 %copy.12.probs_ref = bf16[16,2]{1,0:T(8,128)(2,1)} copy(bf16[16,2]{0,1:T(2,128)(2,1)} %param.10) | data formatting | bytes 128 | tf_op args[3]
  2.0 1.4 %copy.11.ids_ref = s32[16,2]{1,0:T(8,128)} copy(s32[16,2]{0,1:T(2,128)} %param.9) | data formatting | bytes 256 | tf_op args[2]
  3.3 50.9 %shard_map.102 = (bf16[16,3072]{1,0:T(8,128)(2,1)}, bf16[80,1024]{1,0:T(8,128)(2,1)}, bf16[80,1024]{1,0:T(8,128)(2,1)}, bf16[80,1024]{1,0:T(8,128)(2,1)}, bf16[8...) custom-call(bf16[16,6144]{1,0:T(8,128)(2,1)} %tok_ref.1, bf16[16,6144]{1,0:T(8,128)(2,1)} %grad_ref.1, ...), custom_call_target="tpu_custom_call" | custom-call | flops 5033164800 | bytes 37748736 | tf_op jit(solution)/shard_map/pallas_call | solution.py:493
  54.2 0.0 copy-start
  54.2 1.2 %copy-done = bf16[80,6144]{1,0:T(8,128)(2,1)S(1)} copy-done((bf16[80,6144]{1,0:T(8,128)(2,1)S(1)}, bf16[80,6144]{1,0:T(8,128)(2,1)}, u32[]{:S(2)}) %copy-start) | copy-done | bytes 983064
  55.4 0.0 copy-start.1
  55.4 1.2 %copy-done.1 = bf16[80,6144]{1,0:T(8,128)(2,1)S(1)} copy-done((bf16[80,6144]{1,0:T(8,128)(2,1)S(1)}, bf16[80,6144]{1,0:T(8,128)(2,1)}, u32[]{:S(2)}) %copy-start.1) | copy-done | bytes 983064
  56.6 0.0 copy-start.2
  56.6 0.9 %copy-done.2 = bf16[80,1024]{1,0:T(8,128)(2,1)S(1)} copy-done((bf16[80,1024]{1,0:T(8,128)(2,1)S(1)}, bf16[80,1024]{1,0:T(8,128)(2,1)}, u32[]{:S(2)}) %copy-start.2) | copy-done | bytes 163864
  57.5 0.0 copy-start.3
  57.5 0.9 %copy-done.3 = bf16[80,1024]{1,0:T(8,128)(2,1)S(1)} copy-done((bf16[80,1024]{1,0:T(8,128)(2,1)S(1)}, bf16[80,1024]{1,0:T(8,128)(2,1)}, u32[]{:S(2)}) %copy-start.3) | copy-done | bytes 163864
  58.5 0.0 copy-start.4
  58.5 0.9 %copy-done.4 = bf16[80,1024]{1,0:T(8,128)(2,1)S(1)} copy-done((bf16[80,1024]{1,0:T(8,128)(2,1)S(1)}, bf16[80,1024]{1,0:T(8,128)(2,1)}, u32[]{:S(2)}) %copy-start.4) | copy-done | bytes 163864
  59.4 15.2 %shard_map.103 = (bf16[6144,1024]{1,0:T(8,128)(2,1)}, bf16[6144,1024]{1,0:T(8,128)(2,1)}, bf16[1024,6144]{1,0:T(8,128)(2,1)}) custom-call(bf16[80,6144]{1,0:T(8,128)(2,1)S(1)} %copy-done, bf16[80,6144]{1,0:T(8,128)(2,1)S(1)} %copy-done.1, bf16[80,1024]{1,0:T(8,128)(2,1)S(1)} %copy-done.2, bf16[80,1024]{1,0:T(8,128)(2,1)S(1)} %copy-done.3, ...), custom_call_target="tpu_custom_call" | custom-call | flops 3019898880 | bytes 37748736 | tf_op jit(solution)/shard_map/pallas_call | solution.py:544
  74.5 1.5 %copy.14 = bf16[16,3072]{1,0:T(8,128)(2,1)} copy(bf16[16,3072]{1,0:T(8,128)(2,1)} %get-tuple-element.26) | data formatting | bytes 196608
Async XLA Ops:
  54.2 1.2 %copy-start = (bf16[80,6144]{1,0:T(8,128)(2,1)S(1)}, bf16[80,6144]{1,0:T(8,128)(2,1)}, u32[]{:S(2)}) copy-start(bf16[80,6144]{1,0:T(8,128)(2,1)} %get-tuple-element.14.tokx_ref) | copy-start | bytes 2949124
  55.4 1.2 %copy-start.1 = (bf16[80,6144]{1,0:T(8,128)(2,1)S(1)}, bf16[80,6144]{1,0:T(8,128)(2,1)}, u32[]{:S(2)}) copy-start(bf16[80,6144]{1,0:T(8,128)(2,1)} %get-tuple-element.15.gradx_ref) | copy-start | bytes 2949124
  56.6 0.9 %copy-start.2 = (bf16[80,1024]{1,0:T(8,128)(2,1)S(1)}, bf16[80,1024]{1,0:T(8,128)(2,1)}, u32[]{:S(2)}) copy-start(bf16[80,1024]{1,0:T(8,128)(2,1)} %get-tuple-element.16.dg_ref) | copy-start | bytes 491524
  57.5 0.9 %copy-start.3 = (bf16[80,1024]{1,0:T(8,128)(2,1)S(1)}, bf16[80,1024]{1,0:T(8,128)(2,1)}, u32[]{:S(2)}) copy-start(bf16[80,1024]{1,0:T(8,128)(2,1)} %get-tuple-element.17.du_ref) | copy-start | bytes 491524
  58.5 0.9 %copy-start.4 = (bf16[80,1024]{1,0:T(8,128)(2,1)S(1)}, bf16[80,1024]{1,0:T(8,128)(2,1)}, u32[]{:S(2)}) copy-start(bf16[80,1024]{1,0:T(8,128)(2,1)} %get-tuple-element.18.sc_ref) | copy-start | bytes 491524

commit v2 on v1

--- a/solution.py
+++ b/solution.py
@@ -109,6 +109,11 @@
     wu_hbm,
     wd_hbm,
     out_ref,
+    dg_hbm,
+    du_hbm,
+    sc_hbm,
+    tokx_hbm,
+    gradx_hbm,
     dg_ref,
     du_ref,
     sc_ref,
@@ -138,6 +143,7 @@
     red_send,
     red_recv,
     fin_sem,
+    keep_sem,
 ):
     seq_count = EXP_WIN * group
     rows_own, width = tok_ref.shape
@@ -165,6 +171,19 @@
             ),
         )
 
+    kept = [
+        pltpu.make_async_copy(source, target, keep_sem.at[k])
+        for k, (source, target) in enumerate(
+            (
+                (tokx_ref, tokx_hbm),
+                (gradx_ref, gradx_hbm),
+                (dg_ref, dg_hbm),
+                (du_ref, du_hbm),
+                (sc_ref, sc_hbm),
+            )
+        )
+    ]
+
     def order(t):
         return ((h + t // PIECES) % 2) * PIECES + t % PIECES
 
@@ -198,15 +217,16 @@
 
     below = (iota((rows_own, rows_own), 1) < iota((rows_own, rows_own), 0)).astype(BF16)
 
+    diagonal = iota((rows_own, rows_own), 1) == iota((rows_own, rows_own), 0)
+
     def chosen(expert):
-        weight = jnp.zeros((rows_own, 1), F32)
-        hit = jnp.zeros((rows_own, 1), F32)
-        for pick in range(TOPK):
-            same = ids_ref[:, pick : pick + 1] == expert
-            hit = hit + jnp.where(same, 1.0, 0.0)
-            weight = weight + jnp.where(
-                same, probs_ref[:, pick : pick + 1].astype(F32), 0.0
-            )
+        same = ids_ref[...] == expert
+        hit_line = jnp.sum(jnp.where(same, 1.0, 0.0), axis=0, keepdims=True)
+        weight_line = jnp.sum(
+            jnp.where(same, probs_ref[...].astype(F32), 0.0), axis=0, keepdims=True
+        )
+        hit = jnp.sum(jnp.where(diagonal, hit_line, 0.0), axis=1, keepdims=True)
+        weight = jnp.sum(jnp.where(diagonal, weight_line, 0.0), axis=1, keepdims=True)
         spread = jnp.broadcast_to(hit, (rows_own, LANES)).astype(BF16)
         place = dot(below, spread)[:, 0:1]
         place = jnp.where(hit > 0.0, place, -1.0)
@@ -234,11 +254,9 @@
     place_mine, weight_mine = chosen(mine)
     place_other, weight_other = chosen(other)
     mir[0] = token_slab(place_other, weight_other).astype(BF16)
-    mir[1] = slab_of(grad_ref, place_other).astype(BF16)
     own_rows = pl.ds(pl.multiple_of(2 * SLAB * c + SLAB * mine, SLAB), SLAB)
     mir_rows = pl.ds(pl.multiple_of(2 * SLAB * c + SLAB * other, SLAB), SLAB)
     slabs[0, h, own_rows, :] = token_slab(place_mine, weight_mine).astype(BF16)
-    slabs[1, h, own_rows, :] = slab_of(grad_ref, place_mine).astype(BF16)
 
     pl.semaphore_wait(barrier, group + 1)
 
@@ -291,8 +309,10 @@
         )
 
     mirror_copy(0, own_rows).start()
+    send_all(0, 0)
+    mir[1] = slab_of(grad_ref, place_other).astype(BF16)
     mirror_copy(1, own_rows).start()
-    send_all(0, 0)
+    slabs[1, h, own_rows, :] = slab_of(grad_ref, place_mine).astype(BF16)
     mirror_copy(0, mir_rows).wait_recv()
     send_all(0, 1)
     send_all(1, 0)
@@ -342,9 +362,11 @@
     pair_copy(1, h).start()
     pair_copy(0, 1 - h).wait_recv()
     lax.fori_loop(PIECES, 2 * PIECES, forward_step, 0)
+    kept[0].start()
     lax.fori_loop(0, PIECES, back_step, 0)
     pair_copy(1, 1 - h).wait_recv()
     lax.fori_loop(PIECES, 2 * PIECES, back_step, 0)
+    kept[1].start()
 
     gate_pre, up_pre = gate[...], up[...]
     sig = 1.0 / (1.0 + jnp.exp(-gate_pre))
@@ -355,6 +377,8 @@
         hidden_grad * up_pre * (sig * (1.0 + gate_pre * (1.0 - sig)))
     ).astype(BF16)
     du_ref[...] = (hidden_grad * act).astype(BF16)
+    for copy in kept[2:]:
+        copy.start()
 
     cuts = packed.shape[0]
     cut = piece_w // cuts
@@ -469,13 +493,22 @@
     for q in range(cuts):
         part_copy(q).wait_send()
         final_copy(q).wait_send()
-
-
-def weight_grads(tokx_ref, gradx_ref, dg_ref, du_ref, sc_ref, gg_ref, gu_ref, gd_ref):
-    x = tokx_ref[...]
-    gg_ref[...] = row_contract(x, dg_ref[...]).astype(BF16)
-    gu_ref[...] = row_contract(x, du_ref[...]).astype(BF16)
-    gd_ref[...] = row_contract(sc_ref[...], gradx_ref[...]).astype(BF16)
+    for copy in kept:
+        copy.wait()
+
+
+def weight_grads(
+    gt_ref, tokx_ref, gradx_ref, dg_ref, du_ref, sc_ref, gto_ref, gg_ref, gu_ref, gd_ref, sct
+):
+    @pl.when(pl.program_id(0) == 0)
+    def _():
+        gto_ref[...] = gt_ref[...]
+        sct[...] = sc_ref[...].T
+
+    xt = tokx_ref[...].T
+    gg_ref[...] = dot(xt, dg_ref[...]).astype(BF16)
+    gu_ref[...] = dot(xt, du_ref[...]).astype(BF16)
+    gd_ref[...] = dot(sct[...], gradx_ref[...]).astype(BF16)
 
 
 def paired_shards(group, tokens, out_grad, expert_ids, route_probs, w_gate, w_up, w_down):
@@ -501,8 +534,13 @@
             wide,
         ),
         in_specs=[vmem] * 4 + [hbm] * 3,
-        out_specs=(vmem,) * 6,
+        out_specs=(vmem,) + (hbm,) * 5,
         scratch_shapes=[
+            pltpu.VMEM((rows, hidden), BF16),
+            pltpu.VMEM((rows, hidden), BF16),
+            pltpu.VMEM((rows, hidden), BF16),
+            pltpu.VMEM((rows, width), BF16),
+            pltpu.VMEM((rows, width), BF16),
             pltpu.VMEM((2 * PIECES, piece_w, hidden), BF16),
             pltpu.VMEM((2 * PIECES, piece_w, hidden), BF16),
             pltpu.VMEM((2 * PIECES, hidden, piece_w), BF16),
@@ -527,6 +565,7 @@
             dma((cuts, group)),
             dma((cuts, group)),
             dma((2, cuts)),
+            dma((5,)),
         ],
         compiler_params=pltpu.CompilerParams(
             collective_id=0, has_side_effects=True, vmem_limit_bytes=60 * 2**20
@@ -536,33 +575,36 @@
             bytes_accessed=6 * width * hidden,
             transcendentals=rows * hidden,
         ),
-    )(tokens, out_grad, expert_ids, route_probs, w_gate, w_up, w_down)
+    )(tokens, out_grad, expert_ids.T, route_probs.T, w_gate, w_up, w_down)
 
     step = piece_w // 2
     whole = pl.BlockSpec((rows, hidden), lambda i: (0, 0))
     strip = pl.BlockSpec((rows, step), lambda i: (0, i))
-    grad_gate, grad_up, grad_down = pl.pallas_call(
+    whole_gt = pl.BlockSpec(grad_tokens.shape, lambda i: (0, 0))
+    return pl.pallas_call(
         weight_grads,
         grid=(width // step,),
         out_shape=(
+            jax.ShapeDtypeStruct(grad_tokens.shape, BF16),
             jax.ShapeDtypeStruct((width, hidden), BF16),
             jax.ShapeDtypeStruct((width, hidden), BF16),
             jax.ShapeDtypeStruct((hidden, width), BF16),
         ),
-        in_specs=[strip, strip, whole, whole, whole],
+        in_specs=[whole_gt, strip, strip, whole, whole, whole],
         out_specs=(
+            whole_gt,
             pl.BlockSpec((step, hidden), lambda i: (i, 0)),
             pl.BlockSpec((step, hidden), lambda i: (i, 0)),
             pl.BlockSpec((hidden, step), lambda i: (0, i)),
         ),
-        compiler_params=pltpu.CompilerParams(vmem_limit_bytes=48 * 2**20),
+        scratch_shapes=[pltpu.VMEM((hidden, rows), BF16)],
+        compiler_params=pltpu.CompilerParams(vmem_limit_bytes=62 * 2**20),
         cost_estimate=pl.CostEstimate(
             flops=6 * rows * width * hidden,
             bytes_accessed=6 * width * hidden,
             transcendentals=0,
         ),
-    )(tok_x, grad_x, d_gate, d_up, scaled)
-    return grad_tokens, grad_gate, grad_up, grad_down
+    )(grad_tokens, tok_x, grad_x, d_gate, d_up, scaled)
 
 
 def solution(mesh):

time: 76.4 us -> 66.8 us (0.87)
  local copies, waits for them, and re-layouts: 9.36 us -> 0 us
  Pallas kernels: 66.1 us -> 65.3 us
    unnamed x13 -> x0, local copies, waits for them, and re-layouts: 9.36 us -> none
    pallas_call x1, Pallas kernels: 50.9 us -> 50.1 us  [paired_shards(): pl.pallas_call(functools.partial(layer_kernel, group), out_shape=(jax.Sha...]
where the time goes in v2:
time: 66.8 us; the launch traced here: 66 us
  Pallas kernels  65.3 us (98%)
    pallas_call x1, Pallas kernels, paired_shards(): pl.pallas_call(functools.partial(layer_kernel, group), out_shape=(jax.Sha...  50.1 us
    pallas_call x1, Pallas kernels, paired_shards(): pl.pallas_call(weight_grads, grid=(width // step,), out_shape=(jax.ShapeD...  15.2 us

profile of v2, /device:TPU:0, one launch (start us, length us, event | category | flops | bytes accessed | tf_op | source)
XLA Modules:
  0.0 66.0 jit_solution(9656723549013739486)
XLA Ops:
  0.6 50.1 %shard_map.102 = (bf16[16,3072]{1,0:T(8,128)(2,1)}, bf16[80,1024]{1,0:T(8,128)(2,1)}, bf16[80,1024]{1,0:T(8,128)(2,1)}, bf16[80,1024]{1,0:T(8,128)(2,1)}, bf16[8...) custom-call(bf16[16,6144]{1,0:T(8,128)(2,1)} %tok_ref.1, bf16[16,6144]{1,0:T(8,128)(2,1)} %grad_ref.1, s32[2,16]{1,0:T(2,128)} %bitcast.2, ...), custom_call_target="tpu_custom_call" | custom-call | flops 5033164800 | bytes 37748736 | tf_op jit(solution)/shard_map/pallas_call | solution.py:526
  50.7 15.2 %shard_map.103 = (bf16[16,3072]{1,0:T(8,128)(2,1)}, bf16[6144,1024]{1,0:T(8,128)(2,1)}, bf16[6144,1024]{1,0:T(8,128)(2,1)}, bf16[1024,6144]{1,0:T(8,128)(2,1)}) custom-call(bf16[16,3072]{1,0:T(8,128)(2,1)} %get-tuple-element.10.gt_ref, bf16[80,6144]{1,0:T(8,128)(2,1)} %get-tuple-element.11.tokx_ref, bf16[80,6144]{1,0:T(8,128)(2,1)} %get-tuple-element.12.gradx_ref, ...), custom_call_target="tpu_custom_call" | custom-call | flops 3019898880 | bytes 37748736 | tf_op jit(solution)/shard_map/pallas_call | solution.py:584
